TPU v7x, 32 devices: a whole 2x2x4 slice. The times are simulated.
32 devices in a mesh: query: 4 (over y, x), context: 8 (over z, core).
Axes of the slice: x: 2, y: 2, z: 4, core: 2. Of those that a mesh axis runs over, the one named last changes fastest.
Arguments:
- queries: bfloat16 [4, 1024, 128], P('query', 'context'), may hold values from -6 to 6
- keys: bfloat16 [1024, 128], P('context'), may hold values from -6 to 6
- values: bfloat16 [1024, 128], P('context'), may hold values from -6 to 6
- out_grad: bfloat16 [4, 1024, 128], P('query', 'context'), may hold values from -6 to 6
- prefix_states: bfloat16 [8, 8256, 128], P('context'), may hold values from -48 to 48
Outputs:
- grad_queries: bfloat16 [4, 1024, 128], P('query', 'context')
- grad_keys: bfloat16 [8, 128, 128], P('context', 'query')
- grad_values: bfloat16 [8, 128, 128], P('context', 'query')
All inputs are finite; a program needn't handle non-finite values.
Results may differ from a plain program's by a relative error of at most 0.014.
Values may be sent and summed in bfloat16 or wider, within the bound.
A program may use at most 192 MiB of HBM per device.

v0:
```python
import jax
import jax.numpy as jnp
import numpy as np
from jax import lax
from jax.sharding import PartitionSpec as P


def carried_in(part, axis, combine, identity):
    count = lax.axis_size(axis)
    place = lax.axis_index(axis)
    ahead = count - 1 - place
    gathered = lax.all_gather(part, axis)
    state = jnp.zeros_like(part) + jnp.asarray(identity, part.dtype)

    def one(hop, state):
        source = count - 1 - hop
        return combine(state, lax.dynamic_index_in_dim(gathered, source, 0, False))

    return lax.fori_loop(0, ahead, one, state)


def pair_tables(model_width):
    first_index, second_index = np.triu_indices(model_width)
    pair_weight = np.where(first_index == second_index, 1.0, np.sqrt(2.0)).astype(np.float32)
    return (first_index.astype(np.int32), second_index.astype(np.int32), pair_weight)


def expand_cols(column_form, first_index, second_index, pair_weight):
    return (column_form[first_index] * column_form[second_index] * pair_weight[:, None]).astype(
        jnp.bfloat16
    )


def pair_grad(
    feature_grad, column_form, first_index, second_index, pair_weight, onehot_first, onehot_second
):
    weighted = feature_grad.astype(jnp.float32) * pair_weight[:, None]
    term_one = (weighted * column_form[second_index]).astype(jnp.bfloat16)
    term_two = (weighted * column_form[first_index]).astype(jnp.bfloat16)
    dims = (((0,), (0,)), ((), ()))
    return lax.dot_general(
        term_one, onehot_first, dims, preferred_element_type=jnp.float32
    ) + lax.dot_general(term_two, onehot_second, dims, preferred_element_type=jnp.float32)


def cross_terms(grad_state, key_rows, value_rows, tables):
    first_index, second_index, pair_weight, onehot_first, onehot_second = tables
    key_cols = key_rows.astype(jnp.float32).T
    expanded_keys = expand_cols(key_cols, first_index, second_index, pair_weight)
    cross_values = lax.dot_general(
        expanded_keys, grad_state, (((0,), (0,)), ((), ())), preferred_element_type=jnp.float32
    )
    key_feature = lax.dot_general(
        grad_state, value_rows, (((1,), (1,)), ((), ())), preferred_element_type=jnp.float32
    ).astype(jnp.bfloat16)
    cross_keys = pair_grad(
        key_feature, key_cols, first_index, second_index, pair_weight, onehot_first, onehot_second
    )
    return jnp.concatenate([cross_keys, cross_values], axis=1)


def add_terms(earlier, later_part):
    return earlier + later_part


def body(queries, keys, values, out_grad, prefix_states):
    query_rows = queries[0]
    grad_rows = out_grad[0]
    prefix = prefix_states[0]
    row_count, model_width = query_rows.shape
    score_scale = 1.0 / (model_width * row_count)
    first_np, second_np, weight_np = pair_tables(model_width)
    feature_count = first_np.shape[0]
    first_index = jnp.asarray(first_np)
    second_index = jnp.asarray(second_np)
    pair_weight = jnp.asarray(weight_np)
    width_range = jnp.arange(model_width, dtype=jnp.int32)
    onehot_first = (first_index[:, None] == width_range[None, :]).astype(jnp.bfloat16)
    onehot_second = (second_index[:, None] == width_range[None, :]).astype(jnp.bfloat16)
    block_size = min(256, row_count)
    block_total = row_count // block_size
    group_count = lax.axis_size("query")
    group_index = lax.axis_index("query")
    part_rows = row_count // group_count
    share_rows = feature_count // group_count
    share_start = group_index * share_rows

    def state_step(running, pieces):
        query_piece, grad_piece = pieces
        query_cols = query_piece.astype(jnp.float32).T
        query_feature = lax.dot_general(
            prefix, grad_piece, (((1,), (1,)), ((), ())), preferred_element_type=jnp.float32
        ).astype(jnp.bfloat16)
        cross_query = score_scale * pair_grad(
            query_feature,
            query_cols,
            first_index,
            second_index,
            pair_weight,
            onehot_first,
            onehot_second,
        )
        return (running, cross_query)

    summed, cross_pieces = lax.scan(
        state_step,
        jnp.zeros((1, model_width), jnp.float32),
        (
            query_rows.reshape(block_total, block_size, model_width),
            grad_rows.reshape(block_total, block_size, model_width),
        ),
    )
    cross_query = cross_pieces.reshape(row_count, model_width)
    causal = jnp.arange(row_count)[None, :] <= jnp.arange(row_count)[:, None]
    score_dot = lax.dot_general(
        query_rows, keys, (((1,), (1,)), ((), ())), preferred_element_type=jnp.float32
    )
    grad_dot = lax.dot_general(
        grad_rows, values, (((1,), (1,)), ((), ())), preferred_element_type=jnp.float32
    )
    attn = jnp.where(causal, score_scale * score_dot * score_dot, 0.0).astype(jnp.bfloat16)
    slope = jnp.where(causal, 2.0 * score_scale * score_dot * grad_dot, 0.0).astype(jnp.bfloat16)
    local_query = jnp.dot(slope, keys, preferred_element_type=jnp.float32)
    grad_queries = (local_query + cross_query).astype(jnp.bfloat16)[None]
    first_dims = (((0,), (0,)), ((), ()))
    key_local = lax.dot_general(slope, query_rows, first_dims, preferred_element_type=jnp.float32)
    value_local = lax.dot_general(attn, grad_rows, first_dims, preferred_element_type=jnp.float32)
    local_pair = jnp.concatenate([key_local, value_local], axis=1)
    share_tables = (
        lax.dynamic_slice_in_dim(first_index, share_start, share_rows),
        lax.dynamic_slice_in_dim(second_index, share_start, share_rows),
        lax.dynamic_slice_in_dim(pair_weight, share_start, share_rows),
        lax.dynamic_slice_in_dim(onehot_first, share_start, share_rows),
        lax.dynamic_slice_in_dim(onehot_second, share_start, share_rows),
    )
    cross_rows = jnp.zeros((part_rows, 2 * model_width), jnp.float32)
    share_first, share_second, share_weight = (share_tables[0], share_tables[1], share_tables[2])
    query_piece = lax.all_gather(queries, "query", axis=0, tiled=True)
    grad_piece = lax.all_gather(out_grad, "query", axis=0, tiled=True)
    token_rows = query_piece.shape[0] * query_piece.shape[1]
    query_cols = query_piece.reshape(token_rows, model_width).astype(jnp.float32).T
    expanded = expand_cols(query_cols, share_first, share_second, share_weight)
    gathered_sum = jnp.zeros((share_rows, model_width), jnp.float32) + jnp.dot(
        expanded, grad_piece.reshape(token_rows, model_width), preferred_element_type=jnp.float32
    )
    state_share = score_scale * gathered_sum
    later_part = carried_in(state_share, "context", add_terms, jnp.zeros_like(state_share))
    local_pair = local_pair + cross_terms(
        later_part.astype(jnp.bfloat16), keys, values, share_tables
    )
    summed_pair = (
        lax.psum_scatter(
            local_pair.astype(jnp.bfloat16), "query", scatter_dimension=0, tiled=True
        ).astype(jnp.float32)
        + cross_rows
    )
    grad_keys = summed_pair[:, :model_width].astype(jnp.bfloat16)[None]
    grad_values = summed_pair[:, model_width:].astype(jnp.bfloat16)[None]
    return (grad_queries, grad_keys, grad_values)


def solution(mesh):
    return jax.shard_map(
        body,
        mesh=mesh,
        in_specs=(
            P("query", "context", None),
            P("context", None),
            P("context", None),
            P("query", "context", None),
            P("context", None, None),
        ),
        out_specs=(
            P("query", "context", None),
            P("context", "query", None),
            P("context", "query", None),
        ),
        check_vma=False,
    )
```

profile of v0, /device:TPU:0, one launch (start us, length us, event | category | flops | bytes accessed | tf_op | source)
XLA Modules:
  0.0 176.2 jit_solution(16727901461151427162)
XLA Ops:
  8.2 10.1 %all_gather.12 = bf16[4,128,128]{2,1,0:T(8,128)(2,1)S(1)} all-gather(bf16[1,128,128]{2,1,0:T(8,128)(2,1)} %param.10), channel_id=1, replica_groups=mesh['query'=4,'context'=8] {'query'}, dimensions={0}, use_global_device_ids=true | all-gather | bytes 163840 | tf_op jit(solution)/shard_map/all_gather | solution.py:138
  18.5 6.8 %gather_fusion.2 = f32[2064,512]{1,0:T(8,128)} fusion(f32[128,512]{1,0:T(8,128)S(1)} %bitcast.44, s32[3072]{0:T(1024)S(1)} %pad_clamp_fusion.3), kind=kCustom, calls=%fused_computation.2 | custom fusion | bytes 8462400 | tf_op jit(solution)/shard_map/gather | solution.py:29
  25.3 6.7 %gather_fusion.3 = f32[2064,512]{1,0:T(8,128)} fusion(f32[128,512]{1,0:T(8,128)S(1)} %bitcast.45, s32[3072]{0:T(1024)S(1)} %pad_clamp_fusion.2), kind=kCustom, calls=%fused_computation.3 | custom fusion | bytes 8462400 | tf_op jit(solution)/shard_map/gather | solution.py:29
  32.1 8.2 %all_gather.13 = bf16[4,128,128]{2,1,0:T(8,128)(2,1)S(1)} all-gather(bf16[1,128,128]{2,1,0:T(8,128)(2,1)S(1)} %copy-done.4), channel_id=1, replica_groups=mesh['query'=4,'context'=8] {'query'}, dimensions={0}, use_global_device_ids=true | all-gather | bytes 163840 | tf_op jit(solution)/shard_map/all_gather | solution.py:139
  40.3 5.3 %convolution_multiply_fusion = f32[2064,128]{1,0:T(8,128)} fusion(bf16[512,128]{1,0:T(8,128)(2,1)S(1)} %bitcast.49, f32[2064,512]{1,0:T(8,128)} %gather_fusion.2, f32[2064,512]{1,0:T(8,128)} %gather_fusion.3, f32[2064]{0:T(1024)S(1)} %dynamic_slice.29), kind=kOutput, calls=%fused_computation.15 | convolution fusion | flops 273967104 | bytes 9650240 | tf_op jit(solution)/shard_map/dot_general | solution.py:143
  45.8 5.0 %gather_fusion.4 = f32[2064,128]{1,0:T(8,128)} fusion(f32[128,128]{1,0:T(8,128)S(1)} %convert_bitcast_fusion, s32[3072]{0:T(1024)S(1)} %pad_clamp_fusion.2), kind=kCustom, calls=%fused_computation.4 | custom fusion | bytes 2121792 | tf_op jit(solution)/shard_map/gather | solution.py:38
  50.8 5.0 %gather_fusion.5 = f32[2064,128]{1,0:T(8,128)} fusion(f32[128,128]{1,0:T(8,128)S(1)} %convert_bitcast_fusion, s32[3072]{0:T(1024)S(1)} %pad_clamp_fusion.3), kind=kCustom, calls=%fused_computation.5 | custom fusion | bytes 2121792 | tf_op jit(solution)/shard_map/gather | solution.py:39
  56.0 16.3 %gather_fusion = f32[8256,128]{1,0:T(8,128)} fusion(f32[128,128]{1,0:T(8,128)S(1)} %convert_bitcast_fusion.1, s32[9216]{0:T(1024)S(1)} %pad_clamp_fusion.1), kind=kCustom, calls=%fused_computation | custom fusion | bytes 8487168 | tf_op jit(solution)/shard_map/while/body/eval_jaxpr/gather | solution.py:38
  72.3 16.3 %gather_fusion.1 = f32[8256,128]{1,0:T(8,128)} fusion(f32[128,128]{1,0:T(8,128)S(1)} %convert_bitcast_fusion.1, s32[9216]{0:T(1024)S(1)} %pad_clamp_fusion), kind=kCustom, calls=%fused_computation.1 | custom fusion | bytes 8487168 | tf_op jit(solution)/shard_map/while/body/eval_jaxpr/gather | solution.py:39
  89.5 3.7 %fusion.1 = f32[8256,128]{1,0:T(8,128)S(1)} fusion(bf16[1,8256,128]{2,1,0:T(8,128)(2,1)S(1)} %copy-done, f32[8256]{0:T(1024)S(1)} %copy-done.9, bf16[1,128,128]{2,1,0:T(8,128)(2,1)S(1)} %copy-done.4), kind=kOutput, calls=%fused_computation.9 | convolution fusion | flops 273702912 | bytes 6406400 | tf_op jit(solution)/shard_map/while/body/eval_jaxpr/dot_general | solution.py:91
  93.3 2.1 %fusion.4 = f32[128,128]{1,0:T(8,128)S(1)} fusion(f32[8256,128]{1,0:T(8,128)S(1)} %fusion.1, f32[8256,128]{1,0:T(8,128)S(1)} %bitcast.47, s32[8256]{0:T(1024)S(1)} %copy-done.7), kind=kOutput, calls=%fused_computation.19 | convolution fusion | flops 273702912 | bytes 8552704 | tf_op jit(solution)/shard_map/while/body/eval_jaxpr/dot_general | solution.py:41
  95.4 4.5 %iota_compare_fusion.1 = pred[8256,128]{1,0:T(8,128)(4,1)} fusion(s32[8256]{0:T(1024)S(1)} %copy-done.7), kind=kLoop, calls=%fused_computation.13 | loop fusion | flops 1056768 | bytes 1089792 | tf_op jit(solution)/shard_map/eq | solution.py:78
  99.8 4.5 %iota_compare_fusion = pred[8256,128]{1,0:T(8,128)(4,1)} fusion(s32[8256]{0:T(1024)S(1)} %copy-done.6), kind=kLoop, calls=%fused_computation.11 | loop fusion | flops 1056768 | bytes 1089792 | tf_op jit(solution)/shard_map/eq | solution.py:79
  104.3 24.3 %all-gather.3.cloned.1.call-done = f32[16512,128]{1,0:T(8,128)} async-done(((f32[2064,128]{1,0:T(8,128)}), f32[16512,128]{1,0:T(8,128)}) %all-gather.3.cloned.1.call-update) | async-done | bytes 8454160 | tf_op jit(solution)/shard_map/all_gather | solution.py:12
  128.7 10.4 %while.16 = (s32[]{:T(128)}, f32[2064,128]{1,0:T(8,128)S(1)}, s32[]{:T(128)}, f32[8,2064,128]{2,1,0:T(8,128)}, s32[]{:T(128)}, /*index=5*/s32[]{:T(128)}, s32[]{:T(128)}, s32[]{:T(128)}) while((s32[]{:T(128)}, f32[2064,128]{1,0:T(8,128)S(1)}, s32[]{:T(128)}, f32[8,2064,128]{2,1,0:T(8,128)}, s32[]{:T(128)}, /*index=5*/s32[]{:T(128)}, ...), condition=%wide.region_1.2_spmd, body=%wide.region_0.1_spmd.sunk | while | flops 264198 | bytes 3170439 | solution.py:19
  128.7 1.5 bitcast_add_fusion.2
  131.7 1.5 bitcast_add_fusion.2
  133.2 1.5 bitcast_add_fusion.2
  134.7 1.5 bitcast_add_fusion.2
  136.1 1.5 bitcast_add_fusion.2
  137.6 1.5 bitcast_add_fusion.2
  141.3 1.5 fusion.16
  145.1 7.9 %fusion.14 = bf16[1,128,128]{2,1,0:T(8,128)(2,1)} fusion(f32[128,128]{1,0:T(8,128)S(1)} %fusion.41, f32[128,128]{1,0:T(8,128)S(1)} %fusion.4, f32[8256,128]{1,0:T(8,128)} %copy-done.1, f32[8256,128]{1,0:T(8,128)} %gather_fusion.1, s32[8256]{0:T(1024)S(1)} %copy-done.6), kind=kOutput, calls=%fused_computation.31 | convolution fusion | flops 273768448 | bytes 8651008 | tf_op jit(solution)/shard_map/while/body/eval_jaxpr/dot_general | solution.py:43
  153.0 14.1 %reduce-scatter.4.cloned.1.call-done = bf16[32,256]{1,0:T(8,128)(2,1)} async-done(((bf16[128,256]{1,0:T(8,128)(2,1)}), bf16[32,256]{1,0:T(8,128)(2,1)}) %reduce-scatter.4.cloned.1.call-update) | async-done | bytes 16400
  (60 shorter events, 10.8 us)
Async XLA Ops:
  7.2 82.3 %copy-start = (bf16[1,8256,128]{2,1,0:T(8,128)(2,1)S(1)}, bf16[1,8256,128]{2,1,0:T(8,128)(2,1)}, u32[]{:S(2)}) copy-start(bf16[1,8256,128]{2,1,0:T(8,128)(2,1)} %param.14) | copy-start | bytes 6340612
  7.2 121.4 %all-gather.3.cloned.1.call-start = ((), (), s32[]{:S(2)}) async-start(), calls=%async_computation.1 | async-start | bytes 9510912 | tf_op jit(solution)/shard_map/all_gather | solution.py:12
  25.2 6.8 %copy-start.9 = (f32[8256]{0:T(1024)S(1)}, f32[8256]{0:T(1024)}, u32[]{:S(2)}) copy-start(f32[8256]{0:T(1024)} %constant.74.clone) | copy-start | bytes 99076
  25.2 6.8 %copy-start.4 = (bf16[1,128,128]{2,1,0:T(8,128)(2,1)S(1)}, bf16[1,128,128]{2,1,0:T(8,128)(2,1)}, u32[]{:S(2)}) copy-start(bf16[1,128,128]{2,1,0:T(8,128)(2,1)} %param.13) | copy-start | bytes 98308
  40.3 5.3 %copy-start.8 = (bf16[128,128]{1,0:T(8,128)(2,1)S(1)}, bf16[128,128]{1,0:T(8,128)(2,1)}, u32[]{:S(2)}) copy-start(bf16[128,128]{1,0:T(8,128)(2,1)} %param.11) | copy-start | bytes 98308
  45.6 121.5 %reduce-scatter.4.cloned.1.call-start = ((), (), s32[]{:S(2)}) async-start(), calls=%async_computation.2 | async-start | bytes 81920
  50.8 5.0 %copy-start.5 = (bf16[1,128,128]{2,1,0:T(8,128)(2,1)S(1)}, bf16[1,128,128]{2,1,0:T(8,128)(2,1)}, u32[]{:S(2)}) copy-start(bf16[1,128,128]{2,1,0:T(8,128)(2,1)} %param.10) | copy-start | bytes 98308
  50.8 5.1 %copy-start.6 = (s32[8256]{0:T(1024)S(1)}, s32[8256]{0:T(1024)}, u32[]{:S(2)}) copy-start(s32[8256]{0:T(1024)} %constant.73.clone) | copy-start | bytes 99076
  56.0 16.3 %copy-start.7 = (s32[8256]{0:T(1024)S(1)}, s32[8256]{0:T(1024)}, u32[]{:S(2)}) copy-start(s32[8256]{0:T(1024)} %constant.72.clone) | copy-start | bytes 99076
  72.3 16.4 %copy-start.10 = (bf16[128,128]{1,0:T(8,128)(2,1)S(1)}, bf16[128,128]{1,0:T(8,128)(2,1)}, u32[]{:S(2)}) copy-start(bf16[128,128]{1,0:T(8,128)(2,1)} %param.12) | copy-start | bytes 98308
  88.7 4.5 %slice-start = ((s8[4227072]{0:T(1024)(128)(4,1)}), s8[4194304]{0:T(1024)(128)(4,1)S(1)}, s32[]{:S(2)}) async-start(s8[4227072]{0:T(1024)(128)(4,1)} %bitcast.46), calls=%async_computation.3 | async-start | bytes 8388608
  89.5 3.8 %slice-start.1 = ((s8[4227072]{0:T(1024)(128)(4,1)}), s8[32768]{0:T(1024)(128)(4,1)S(1)}, s32[]{:S(2)}) async-start(s8[4227072]{0:T(1024)(128)(4,1)} %bitcast.46), calls=%async_computation.4 | async-start | bytes 65536
  93.3 2.1 %copy-start.1 = (f32[8256,128]{1,0:T(8,128)}, f32[8256,128]{1,0:T(8,128)S(1)}, u32[]{:S(2)}) copy-start(f32[8256,128]{1,0:T(8,128)S(1)} %fusion.1) | copy-start | bytes 12681220
  139.1 1.2 copy-start.2
  139.1 1.5 copy-start.3
Sparse Core Ops, SparseCore 0:
  45.7 82.8 all-gather.2
  145.2 21.8 reduce-scatter.3
where the time goes:
time: 177 us; the launch traced here: 176 us
  local copies, waits for them, and re-layouts  60.8 us (34%)
  waiting for transfers between devices  38.5 us (22%)
  matrix products  23.9 us (14%)
  other arithmetic  20.2 us (11%)
  blocking collectives  18.3 us (10%)
  between operations  14.3 us (8%)
    all_gather x1, waiting for transfers between devices, carried_in(): gathered = lax.all_gather(part, axis)  24.3 us
    gather x2, local copies, waits for them, and re-layouts, pair_grad(): term_one = (weighted * column_form[second_index]).astype(jnp.bfloat16)  21.3 us
    gather x2, local copies, waits for them, and re-layouts, pair_grad(): term_two = (weighted * column_form[first_index]).astype(jnp.bfloat16)  21.3 us
    unnamed x3, waiting for transfers between devices  14.2 us
    add x7, other arithmetic, add_terms(): return earlier + later_part  10.2 us
    all_gather x1, blocking collectives, body(): query_piece = lax.all_gather(queries, 'query', axis=0, tiled=True)  10.1 us
    dot_general x2, matrix products, pair_grad(): lax.dot_general(term_two, onehot_second, dims, preferred_element_type=jnp...  9.35 us
    all_gather x1, blocking collectives, body(): grad_piece = lax.all_gather(out_grad, 'query', axis=0, tiled=True)  8.24 us
  transfers between devices with their start and end apart: 2, of which 2 were waited for; matrix products, arithmetic and copies ran while one was open for 38% of the time, Pallas kernels for 0%

commit v1 on v0

v1 whole, which is shorter than its diff:
```python
import functools

import jax
import jax.numpy as jnp
import numpy as np
from jax import lax
from jax.experimental import pallas as pl
from jax.experimental.pallas import tpu as pltpu
from jax.sharding import PartitionSpec as P

MESH = pl.DeviceIdType.MESH
NT = (((1,), (1,)), ((), ()))
NN = (((1,), (0,)), ((), ()))


def dot(a, b, dims):
    return lax.dot_general(a, b, dims, preferred_element_type=jnp.float32)


def chunk_count(features, most=12):
    for count in range(most, 0, -1):
        if features % (16 * count) == 0:
            return count
    return 1


def kernel(
    q_ref, k_ref, v_ref, g_ref, p_ref, dq_ref, dk_ref, dv_ref,
    kk, vv, qb, gb, pb, fb, xt, red, acc, sb, rb,
    local_sem, p_sem, kv_send, kv_recv, z_send, z_recv, x_send, x_recv,
):
    heads = lax.axis_size("query")
    chips = lax.axis_size("context") // 2
    group = 2 * heads
    h = lax.axis_index("query")
    place = lax.axis_index("context")
    z, core = place // 2, place % 2
    me = core * heads + h
    rows, width = q_ref.shape[1], q_ref.shape[2]
    features = p_ref.shape[1]
    scale = 1.0 / (width * rows)
    share = rows // heads
    chunks = chunk_count(features)
    chunk = features // chunks

    loads = [
        pltpu.make_async_copy(q_ref.at[0], qb.at[0], local_sem.at[0]),
        pltpu.make_async_copy(g_ref.at[0], gb.at[0], local_sem.at[1]),
        pltpu.make_async_copy(k_ref, kk.at[core], local_sem.at[2]),
        pltpu.make_async_copy(v_ref, vv.at[core], local_sem.at[3]),
    ]
    for load in loads:
        load.start()
    p_loads = []
    for n in range(chunks):
        part = pl.ds(n * chunk, chunk)
        load = pltpu.make_async_copy(p_ref.at[0, part], pb.at[part], p_sem.at[n])
        load.start()
        p_loads.append(load)

    barrier = pltpu.get_barrier_semaphore()

    def peer(offset):
        other = lax.rem(me + offset, group)
        return {"query": other % heads, "context": 2 * z + other // heads}

    for offset in range(1, group):
        pl.semaphore_signal(barrier, inc=1, device_id=peer(offset), device_id_type=MESH)
    for step in range(1, chips):
        @pl.when(z + step < chips)
        def _():
            pl.semaphore_signal(
                barrier, inc=1, device_id={"context": place + 2 * step}, device_id_type=MESH
            )
    pl.semaphore_wait(barrier, group - 1 + z)

    def down(step):
        return [
            pltpu.make_async_remote_copy(
                src_ref=src.at[0],
                dst_ref=dst.at[step],
                send_sem=z_send.at[which, step],
                recv_sem=z_recv.at[which, step],
                device_id={"context": place - 2 * step},
                device_id_type=MESH,
            )
            for which, (src, dst) in enumerate(((q_ref, qb), (g_ref, gb)))
        ]

    for step in range(chips - 1, 0, -1):
        @pl.when(z >= step)
        def _():
            for copy in down(step):
                copy.start()

    kv = [
        pltpu.make_async_remote_copy(
            src_ref=src,
            dst_ref=dst.at[core],
            send_sem=kv_send.at[which],
            recv_sem=kv_recv.at[which],
            device_id={"context": place + 1 - 2 * core},
            device_id_type=MESH,
        )
        for which, (src, dst) in enumerate(((k_ref, kk), (v_ref, vv)))
    ]
    for copy in kv:
        copy.start()
    for load in loads:
        load.wait()

    q_own, g_own = qb[0], gb[0]
    xt[...] = q_own.astype(jnp.float32).T
    zero = h // heads
    spot = lax.broadcasted_iota(jnp.int32, (8, rows), 0)
    done, filled = 0, 0
    total = jnp.zeros((width, rows), jnp.float32)
    cross = []
    for tile in range(width // 8):
        length = width - 8 * tile
        last = 8 * tile + 8
        need = last * width - last * (last - 1) // 2
        while filled < need:
            p_loads[done].wait()
            part = pl.ds(filled, chunk)
            fb[part, :] = dot(pb[part, :], g_own, NT)
            done, filled = done + 1, filled + chunk
        x_tile = xt[8 * tile:, :]

        def one(r, total, tile=tile, length=length, x_tile=x_tile):
            i = 8 * tile + r
            begin = i * width - (i * (i - 1)) // 2 - r + zero
            feat = fb[pl.ds(begin, length), :]
            weight = jnp.where(spot < r, 0.0, jnp.where(spot == r, np.float32(np.sqrt(0.5)), 1.0))
            head = feat[:8] * weight
            feat = jnp.concatenate([head, feat[8:]], axis=0) if length > 8 else head
            row = xt[pl.ds(i + zero, 1), :]
            red[i] = jnp.sum((feat * x_tile).reshape(length // 8, 8, rows), axis=0)
            return total + feat * row

        total = lax.fori_loop(0, 8, one, total, unroll=8)
        cross.append(total[:8])
        total = total[8:]
    cross_t = jnp.concatenate(cross, axis=0) + jnp.sum(red[...], axis=1)
    cross_q = (scale * np.sqrt(2.0)) * cross_t.T

    for copy in kv:
        copy.wait()
    keys = kk[...].reshape(2 * rows, width)
    vals = vv[...].reshape(2 * rows, width)

    def weights(q, g):
        score = dot(keys, q, NT)
        return scale * score * score, (2.0 * scale) * score * dot(vals, g, NT)

    attn, slope = weights(q_own, g_own)
    key_at = lax.broadcasted_iota(jnp.int32, (2 * rows, rows), 0)
    query_at = lax.broadcasted_iota(jnp.int32, (2 * rows, rows), 1) + core * rows
    causal = key_at <= query_at
    attn = jnp.where(causal, attn, 0.0).astype(jnp.bfloat16)
    slope = jnp.where(causal, slope, 0.0).astype(jnp.bfloat16)
    acc[:, :width] = dot(slope, q_own, NN)
    acc[:, width:] = dot(attn, g_own, NN)
    own_score = dot(q_own, kk[core], NT)
    own_slope = (2.0 * scale) * own_score * dot(g_own, vv[core], NT)
    own_causal = lax.broadcasted_iota(jnp.int32, (rows, rows), 1) <= lax.broadcasted_iota(
        jnp.int32, (rows, rows), 0
    )
    own_slope = jnp.where(own_causal, own_slope, 0.0).astype(jnp.bfloat16)
    dq_ref[0] = (dot(own_slope, kk[core], NN) + cross_q).astype(dq_ref.dtype)

    for step in range(1, chips):
        @pl.when(z + step < chips)
        def _():
            for copy in down(step):
                copy.wait_recv()
            q, g = qb[step], gb[step]
            attn, slope = weights(q, g)
            acc[:, :width] += dot(slope.astype(jnp.bfloat16), q, NN)
            acc[:, width:] += dot(attn.astype(jnp.bfloat16), g, NN)

    sb[...] = acc[...].astype(jnp.bfloat16).reshape(group, share, 2 * width)
    swaps = []
    for offset in range(1, group):
        other = lax.rem(me + offset, group)
        copy = pltpu.make_async_remote_copy(
            src_ref=sb.at[other],
            dst_ref=rb.at[offset],
            send_sem=x_send.at[offset],
            recv_sem=x_recv.at[offset],
            device_id=peer(offset),
            device_id_type=MESH,
        )
        copy.start()
        swaps.append(copy)
    mine = acc[pl.ds(pl.multiple_of(me * share, share), share), :]
    for offset, copy in enumerate(swaps, 1):
        copy.wait_recv()
        mine = mine + rb[offset].astype(jnp.float32)
    dk_ref[0] = mine[:, :width].astype(dk_ref.dtype)
    dv_ref[0] = mine[:, width:].astype(dv_ref.dtype)

    for copy in swaps:
        copy.wait_send()
    for step in range(1, chips):
        @pl.when(z >= step)
        def _():
            for copy in down(step):
                copy.wait_send()


def body(queries, keys, values, out_grad, prefix_states):
    heads = lax.axis_size("query")
    chips = lax.axis_size("context") // 2
    group = 2 * heads
    rows, width = keys.shape
    features = prefix_states.shape[1]
    share = rows // heads
    chunks = chunk_count(features)
    half = jax.ShapeDtypeStruct((1, share, width), jnp.bfloat16)
    dma = pltpu.SemaphoreType.DMA
    return pl.pallas_call(
        kernel,
        out_shape=(jax.ShapeDtypeStruct(queries.shape, jnp.bfloat16), half, half),
        in_specs=[pl.BlockSpec(memory_space=pl.ANY)] * 5,
        out_specs=[pl.BlockSpec(memory_space=pltpu.VMEM)] * 3,
        scratch_shapes=[
            pltpu.VMEM((2, rows, width), jnp.bfloat16),
            pltpu.VMEM((2, rows, width), jnp.bfloat16),
            pltpu.VMEM((chips, rows, width), jnp.bfloat16),
            pltpu.VMEM((chips, rows, width), jnp.bfloat16),
            pltpu.VMEM((features, width), jnp.bfloat16),
            pltpu.VMEM((features, rows), jnp.float32),
            pltpu.VMEM((width, rows), jnp.float32),
            pltpu.VMEM((width, 8, rows), jnp.float32),
            pltpu.VMEM((2 * rows, 2 * width), jnp.float32),
            pltpu.VMEM((group, share, 2 * width), jnp.bfloat16),
            pltpu.VMEM((group, share, 2 * width), jnp.bfloat16),
            dma((4,)),
            dma((chunks,)),
            dma((2,)),
            dma((2,)),
            dma((2, chips)),
            dma((2, chips)),
            dma((group,)),
            dma((group,)),
        ],
        compiler_params=pltpu.CompilerParams(
            collective_id=0, has_side_effects=True, vmem_limit_bytes=32 * 1024 * 1024
        ),
        cost_estimate=pl.CostEstimate(
            flops=2 * features * width * rows, bytes_accessed=2 * features * width, transcendentals=0
        ),
        name="power_backward",
    )(queries, keys, values, out_grad, prefix_states)


def solution(mesh):
    return jax.shard_map(
        body,
        mesh=mesh,
        in_specs=(
            P("query", "context", None),
            P("context", None),
            P("context", None),
            P("query", "context", None),
            P("context", None, None),
        ),
        out_specs=(
            P("query", "context", None),
            P("context", "query", None),
            P("context", "query", None),
        ),
        check_vma=False,
    )
```

time: 177 us -> 26.6 us (0.15)
  local copies, waits for them, and re-layouts: 60.8 us -> 6.43 us
  waiting for transfers between devices: 38.5 us -> 0 us
  matrix products: 23.9 us -> 0 us
  other arithmetic: 20.2 us -> 0 us
  Pallas kernels: 0 us -> 19.1 us
  blocking collectives: 18.3 us -> 0 us
  between operations: 14.3 us -> 0.65 us
    gather x6 -> x0, local copies, waits for them, and re-layouts: 56.1 us -> none  [the longest x2 21.3 us: pair_grad(): term_one = (weighted * column_form[second_index]).astype(jnp.bfloat16)]
    all_gather x1 -> x0, waiting for transfers between devices: 24.3 us -> none  [carried_in(): gathered = lax.all_gather(part, axis)]
    dot_general x13 -> x0, matrix products: 23.9 us -> none  [the longest x2 9.35 us: pair_grad(): lax.dot_general(term_two, onehot_second, dims, preferred_element_type=jnp...]
    pallas_call x0 -> x1, Pallas kernels: none -> 19.1 us  [body(): pl.pallas_call(kernel, out_shape=(jax.ShapeDtypeStruct(queries.shape, jnp...]
    all_gather x2 -> x0, blocking collectives: 18.3 us -> none  [the longest x1 10.1 us: body(): query_piece = lax.all_gather(queries, 'query', axis=0, tiled=True)]
    unnamed x3 -> x0, waiting for transfers between devices: 14.2 us -> none
    add x7 -> x0, other arithmetic: 10.2 us -> none  [add_terms(): return earlier + later_part]
    eq x2 -> x0, other arithmetic: 8.94 us -> none  [the longest x1 4.48 us: body(): first_index[:, None] == width_range[None, :]]
  transfers between devices with their start and end apart: 2 -> 0, of which waited for: 2 -> 0; matrix products, arithmetic and copies ran while one was open for 38% -> 0% of each run, Pallas kernels for 0% -> 0%
where the time goes in v1:
time: 26.6 us; the launch traced here: 26.2 us
  Pallas kernels  19.1 us (72%)
  local copies, waits for them, and re-layouts  6.43 us (24%)
  between operations  0.65 us (2%)
    pallas_call x1, Pallas kernels, body(): pl.pallas_call(kernel, out_shape=(jax.ShapeDtypeStruct(queries.shape, jnp...  19.1 us
    unnamed x13, local copies, waits for them, and re-layouts  6.43 us

profile of v1, /device:TPU:0, one launch (start us, length us, event | category | flops | bytes accessed | tf_op | source)
XLA Modules:
  0.0 26.2 jit_solution(17566964827583778044)
XLA Ops:
  0.6 0.0 copy-start
  0.6 1.6 %copy-done = bf16[1,8256,128]{2,1,0:T(8,128)(2,1)S(1)} copy-done((bf16[1,8256,128]{2,1,0:T(8,128)(2,1)S(1)}, bf16[1,8256,128]{2,1,0:T(8,128)(2,1)}, u32[]{:S(2)}) %copy-start) | copy-done | bytes 2113560
  2.2 0.0 copy-start.1
  2.2 0.8 %copy-done.1 = bf16[1,128,128]{2,1,0:T(8,128)(2,1)S(1)} copy-done((bf16[1,128,128]{2,1,0:T(8,128)(2,1)S(1)}, bf16[1,128,128]{2,1,0:T(8,128)(2,1)}, u32[]{:S(2)}) %copy-start.1) | copy-done | bytes 32792
  3.0 0.0 copy-start.2
  3.0 0.8 %copy-done.2 = bf16[128,128]{1,0:T(8,128)(2,1)S(1)} copy-done((bf16[128,128]{1,0:T(8,128)(2,1)S(1)}, bf16[128,128]{1,0:T(8,128)(2,1)}, u32[]{:S(2)}) %copy-start.2) | copy-done | bytes 32792
  3.7 0.0 copy-start.3
  3.7 0.8 %copy-done.3 = bf16[128,128]{1,0:T(8,128)(2,1)S(1)} copy-done((bf16[128,128]{1,0:T(8,128)(2,1)S(1)}, bf16[128,128]{1,0:T(8,128)(2,1)}, u32[]{:S(2)}) %copy-start.3) | copy-done | bytes 32792
  4.5 0.0 copy-start.4
  4.5 0.8 %copy-done.4 = bf16[1,128,128]{2,1,0:T(8,128)(2,1)S(1)} copy-done((bf16[1,128,128]{2,1,0:T(8,128)(2,1)S(1)}, bf16[1,128,128]{2,1,0:T(8,128)(2,1)}, u32[]{:S(2)}) %copy-start.4) | copy-done | bytes 32792
  5.3 19.1 %power_backward.1 = (bf16[1,128,128]{2,1,0:T(8,128)(2,1)S(1)}, bf16[1,32,128]{2,1,0:T(8,128)(2,1)S(1)}, bf16[1,32,128]{2,1,0:T(8,128)(2,1)S(1)}) custom-call(bf16[1,128,128]{2,1,0:T(8,128)(2,1)S(1)} %copy-done.1, bf16[128,128]{1,0:T(8,128)(2,1)S(1)} %copy-done.2, bf16[128,128]{1,0:T(8,128)(2,1)S(1)} %copy-done.3, bf16[1,128,128]{2,1,0:T(8,128)(2,1)S(1)} %copy-done.4, ...), custom_call_target="tpu_custom_call" | custom-call | flops 270532608 | bytes 2113536 | tf_op jit(solution)/shard_map/power_backward/pallas_call | solution.py:222
  24.4 0.6 %copy.11 = bf16[1,128,128]{2,1,0:T(8,128)(2,1)} copy(bf16[1,128,128]{2,1,0:T(8,128)(2,1)S(1)} %get-tuple-element.6) | data formatting | bytes 65536
  25.0 0.6 %copy.12 = bf16[1,32,128]{2,1,0:T(8,128)(2,1)} copy(bf16[1,32,128]{2,1,0:T(8,128)(2,1)S(1)} %get-tuple-element.7) | data formatting | bytes 16384
  25.6 0.6 %copy.13 = bf16[1,32,128]{2,1,0:T(8,128)(2,1)} copy(bf16[1,32,128]{2,1,0:T(8,128)(2,1)S(1)} %get-tuple-element.8) | data formatting | bytes 16384
Async XLA Ops:
  0.6 1.6 %copy-start = (bf16[1,8256,128]{2,1,0:T(8,128)(2,1)S(1)}, bf16[1,8256,128]{2,1,0:T(8,128)(2,1)}, u32[]{:S(2)}) copy-start(bf16[1,8256,128]{2,1,0:T(8,128)(2,1)} %p_ref.1) | copy-start | bytes 6340612
  2.2 0.8 %copy-start.1 = (bf16[1,128,128]{2,1,0:T(8,128)(2,1)S(1)}, bf16[1,128,128]{2,1,0:T(8,128)(2,1)}, u32[]{:S(2)}) copy-start(bf16[1,128,128]{2,1,0:T(8,128)(2,1)} %q_ref.1) | copy-start | bytes 98308
  3.0 0.8 %copy-start.2 = (bf16[128,128]{1,0:T(8,128)(2,1)S(1)}, bf16[128,128]{1,0:T(8,128)(2,1)}, u32[]{:S(2)}) copy-start(bf16[128,128]{1,0:T(8,128)(2,1)} %k_ref.1) | copy-start | bytes 98308
  3.7 0.8 %copy-start.3 = (bf16[128,128]{1,0:T(8,128)(2,1)S(1)}, bf16[128,128]{1,0:T(8,128)(2,1)}, u32[]{:S(2)}) copy-start(bf16[128,128]{1,0:T(8,128)(2,1)} %v_ref.1) | copy-start | bytes 98308
  4.5 0.8 %copy-start.4 = (bf16[1,128,128]{2,1,0:T(8,128)(2,1)S(1)}, bf16[1,128,128]{2,1,0:T(8,128)(2,1)}, u32[]{:S(2)}) copy-start(bf16[1,128,128]{2,1,0:T(8,128)(2,1)} %g_ref.1) | copy-start | bytes 98308

commit v2 on v1

--- a/solution.py
+++ b/solution.py
@@ -17,7 +17,7 @@
     return lax.dot_general(a, b, dims, preferred_element_type=jnp.float32)
 
 
-def chunk_count(features, most=12):
+def chunk_count(features, most=4):
     for count in range(most, 0, -1):
         if features % (16 * count) == 0:
             return count
@@ -51,12 +51,9 @@
     ]
     for load in loads:
         load.start()
-    p_loads = []
     for n in range(chunks):
         part = pl.ds(n * chunk, chunk)
-        load = pltpu.make_async_copy(p_ref.at[0, part], pb.at[part], p_sem.at[n])
-        load.start()
-        p_loads.append(load)
+        pltpu.make_async_copy(p_ref.at[0, part], pb.at[part], p_sem.at[n]).start()
 
     barrier = pltpu.get_barrier_semaphore()
 
@@ -111,34 +108,33 @@
 
     q_own, g_own = qb[0], gb[0]
     xt[...] = q_own.astype(jnp.float32).T
-    zero = h // heads
     spot = lax.broadcasted_iota(jnp.int32, (8, rows), 0)
-    done, filled = 0, 0
+
+    def expand(n, carry):
+        part = pl.ds(pl.multiple_of(n * chunk, chunk), chunk)
+        pltpu.make_async_copy(p_ref.at[0, part], pb.at[part], p_sem.at[n]).wait()
+        fb[part, :] = dot(pb[part, :], g_own, NT)
+        return carry
+
+    lax.fori_loop(0, chunks, expand, 0)
     total = jnp.zeros((width, rows), jnp.float32)
     cross = []
     for tile in range(width // 8):
         length = width - 8 * tile
-        last = 8 * tile + 8
-        need = last * width - last * (last - 1) // 2
-        while filled < need:
-            p_loads[done].wait()
-            part = pl.ds(filled, chunk)
-            fb[part, :] = dot(pb[part, :], g_own, NT)
-            done, filled = done + 1, filled + chunk
-        x_tile = xt[8 * tile:, :]
-
-        def one(r, total, tile=tile, length=length, x_tile=x_tile):
+
+        def one(r, total, tile=tile, length=length):
             i = 8 * tile + r
-            begin = i * width - (i * (i - 1)) // 2 - r + zero
+            begin = i * width - (i * (i - 1)) // 2 - r
             feat = fb[pl.ds(begin, length), :]
             weight = jnp.where(spot < r, 0.0, jnp.where(spot == r, np.float32(np.sqrt(0.5)), 1.0))
             head = feat[:8] * weight
             feat = jnp.concatenate([head, feat[8:]], axis=0) if length > 8 else head
-            row = xt[pl.ds(i + zero, 1), :]
+            row = xt[pl.ds(i, 1), :]
+            x_tile = xt[8 * tile:, :]
             red[i] = jnp.sum((feat * x_tile).reshape(length // 8, 8, rows), axis=0)
             return total + feat * row
 
-        total = lax.fori_loop(0, 8, one, total, unroll=8)
+        total = lax.fori_loop(0, 8, one, total)
         cross.append(total[:8])
         total = total[8:]
     cross_t = jnp.concatenate(cross, axis=0) + jnp.sum(red[...], axis=1)
@@ -246,7 +242,7 @@
             dma((group,)),
         ],
         compiler_params=pltpu.CompilerParams(
-            collective_id=0, has_side_effects=True, vmem_limit_bytes=32 * 1024 * 1024
+            collective_id=0, has_side_effects=True, vmem_limit_bytes=63 * 1024 * 1024
         ),
         cost_estimate=pl.CostEstimate(
             flops=2 * features * width * rows, bytes_accessed=2 * features * width, transcendentals=0

time: 26.6 us -> 21.9 us (0.82)
  local copies, waits for them, and re-layouts: 6.43 us -> 3.96 us
  Pallas kernels: 19.1 us -> 17 us
    unnamed x13 -> x3, local copies, waits for them, and re-layouts: 6.43 us -> 3.96 us
    pallas_call x1, Pallas kernels: 19.1 us -> 17 us  [body(): pl.pallas_call(kernel, out_shape=(jax.ShapeDtypeStruct(queries.shape, jnp...]
where the time goes in v2:
time: 21.9 us; the launch traced here: 21.6 us
  Pallas kernels  17 us (78%)
  local copies, waits for them, and re-layouts  3.96 us (18%)
  between operations  0.64 us (3%)
    pallas_call x1, Pallas kernels, body(): pl.pallas_call(kernel, out_shape=(jax.ShapeDtypeStruct(queries.shape, jnp...  17 us
    unnamed x3, local copies, waits for them, and re-layouts  3.96 us

profile of v2, /device:TPU:0, one launch (start us, length us, event | category | flops | bytes accessed | tf_op | source)
XLA Modules:
  0.0 21.6 jit_solution(7592572102340720)
XLA Ops:
  0.6 17.0 %power_backward.1 = (bf16[1,128,128]{2,1,0:T(8,128)(2,1)}, bf16[1,32,128]{2,1,0:T(8,128)(2,1)}, bf16[1,32,128]{2,1,0:T(8,128)(2,1)}) custom-call(bf16[1,128,128]{2,1,0:T(8,128)(2,1)} %q_ref.1, bf16[128,128]{1,0:T(8,128)(2,1)} %k_ref.1, bf16[128,128]{1,0:T(8,128)(2,1)} %v_ref.1, bf16[1,128,128]{2,1,0:T(8,128)(2,1)} %g_ref.1, bf16[1,8256,128]{2,1,0:T(8,128)(2,1)} %p_ref.1), custom_call_target="tpu_custom_call" | custom-call | flops 270532608 | bytes 2113536 | tf_op jit(solution)/shard_map/power_backward/pallas_call | solution.py:218
  17.7 1.4 %copy.11 = bf16[1,128,128]{2,1,0:T(8,128)(2,1)} copy(bf16[1,128,128]{2,1,0:T(8,128)(2,1)} %get-tuple-element.6) | data formatting | bytes 65536
  19.1 1.3 %copy.12 = bf16[1,32,128]{2,1,0:T(8,128)(2,1)} copy(bf16[1,32,128]{2,1,0:T(8,128)(2,1)} %get-tuple-element.7) | data formatting | bytes 16384
  20.4 1.3 %copy.13 = bf16[1,32,128]{2,1,0:T(8,128)(2,1)} copy(bf16[1,32,128]{2,1,0:T(8,128)(2,1)} %get-tuple-element.8) | data formatting | bytes 16384

commit v3 on v2

--- a/solution.py
+++ b/solution.py
@@ -24,17 +24,34 @@
     return 1
 
 
+def block_batch(chips, most=4):
+    return max(size for size in range(1, most + 1) if chips % size == 0)
+
+
+def place(dq_in, dkv_in, dq_out, dk_out, dv_out, sems):
+    copies = [
+        pltpu.make_async_copy(src, dst, sems.at[n])
+        for n, (src, dst) in enumerate(
+            ((dq_in, dq_out), (dkv_in.at[0], dk_out.at[0]), (dkv_in.at[1], dv_out.at[0]))
+        )
+    ]
+    for copy in copies:
+        copy.start()
+    for copy in copies:
+        copy.wait()
+
+
 def kernel(
-    q_ref, k_ref, v_ref, g_ref, p_ref, dq_ref, dk_ref, dv_ref,
-    kk, vv, qb, gb, pb, fb, xt, red, acc, sb, rb,
-    local_sem, p_sem, kv_send, kv_recv, z_send, z_recv, x_send, x_recv,
+    q_ref, k_ref, v_ref, g_ref, p_ref, dq_ref, dkv_ref,
+    dqb, dkvb, kk, vv, qb, gb, pb, fb, xt, red, acc, sb, rb,
+    out_sem, local_sem, p_sem, kv_send, kv_recv, z_send, z_recv, x_send, x_recv,
 ):
     heads = lax.axis_size("query")
     chips = lax.axis_size("context") // 2
     group = 2 * heads
     h = lax.axis_index("query")
-    place = lax.axis_index("context")
-    z, core = place // 2, place % 2
+    spot_at = lax.axis_index("context")
+    z, core = spot_at // 2, spot_at % 2
     me = core * heads + h
     rows, width = q_ref.shape[1], q_ref.shape[2]
     features = p_ref.shape[1]
@@ -67,7 +84,7 @@
         @pl.when(z + step < chips)
         def _():
             pl.semaphore_signal(
-                barrier, inc=1, device_id={"context": place + 2 * step}, device_id_type=MESH
+                barrier, inc=1, device_id={"context": spot_at + 2 * step}, device_id_type=MESH
             )
     pl.semaphore_wait(barrier, group - 1 + z)
 
@@ -78,7 +95,7 @@
                 dst_ref=dst.at[step],
                 send_sem=z_send.at[which, step],
                 recv_sem=z_recv.at[which, step],
-                device_id={"context": place - 2 * step},
+                device_id={"context": spot_at - 2 * step},
                 device_id_type=MESH,
             )
             for which, (src, dst) in enumerate(((q_ref, qb), (g_ref, gb)))
@@ -96,13 +113,18 @@
             dst_ref=dst.at[core],
             send_sem=kv_send.at[which],
             recv_sem=kv_recv.at[which],
-            device_id={"context": place + 1 - 2 * core},
+            device_id={"context": spot_at + 1 - 2 * core},
             device_id_type=MESH,
         )
         for which, (src, dst) in enumerate(((k_ref, kk), (v_ref, vv)))
     ]
     for copy in kv:
         copy.start()
+    for step in range(1, chips):
+        @pl.when(z + step >= chips)
+        def _():
+            qb[step] = jnp.zeros((rows, width), jnp.bfloat16)
+            gb[step] = jnp.zeros((rows, width), jnp.bfloat16)
     for load in loads:
         load.wait()
 
@@ -134,7 +156,7 @@
             red[i] = jnp.sum((feat * x_tile).reshape(length // 8, 8, rows), axis=0)
             return total + feat * row
 
-        total = lax.fori_loop(0, 8, one, total)
+        total = lax.fori_loop(0, 8, one, total, unroll=2)
         cross.append(total[:8])
         total = total[8:]
     cross_t = jnp.concatenate(cross, axis=0) + jnp.sum(red[...], axis=1)
@@ -149,31 +171,50 @@
         score = dot(keys, q, NT)
         return scale * score * score, (2.0 * scale) * score * dot(vals, g, NT)
 
-    attn, slope = weights(q_own, g_own)
-    key_at = lax.broadcasted_iota(jnp.int32, (2 * rows, rows), 0)
-    query_at = lax.broadcasted_iota(jnp.int32, (2 * rows, rows), 1) + core * rows
-    causal = key_at <= query_at
-    attn = jnp.where(causal, attn, 0.0).astype(jnp.bfloat16)
-    slope = jnp.where(causal, slope, 0.0).astype(jnp.bfloat16)
-    acc[:, :width] = dot(slope, q_own, NN)
-    acc[:, width:] = dot(attn, g_own, NN)
     own_score = dot(q_own, kk[core], NT)
     own_slope = (2.0 * scale) * own_score * dot(g_own, vv[core], NT)
     own_causal = lax.broadcasted_iota(jnp.int32, (rows, rows), 1) <= lax.broadcasted_iota(
         jnp.int32, (rows, rows), 0
     )
     own_slope = jnp.where(own_causal, own_slope, 0.0).astype(jnp.bfloat16)
-    dq_ref[0] = (dot(own_slope, kk[core], NN) + cross_q).astype(dq_ref.dtype)
-
-    for step in range(1, chips):
+    dqb[0] = (dot(own_slope, kk[core], NN) + cross_q).astype(dqb.dtype)
+    dq_out = pltpu.make_async_copy(dqb, dq_ref, out_sem.at[0])
+    dq_out.start()
+
+    batch = block_batch(chips)
+    key_at = lax.broadcasted_iota(jnp.int32, (2 * rows, batch * rows), 0)
+    query_at = lax.broadcasted_iota(jnp.int32, (2 * rows, batch * rows), 1)
+    causal = key_at <= jnp.where(query_at < rows, query_at + core * rows, 2 * rows)
+
+    def arrive(step):
         @pl.when(z + step < chips)
         def _():
             for copy in down(step):
                 copy.wait_recv()
-            q, g = qb[step], gb[step]
-            attn, slope = weights(q, g)
-            acc[:, :width] += dot(slope.astype(jnp.bfloat16), q, NN)
-            acc[:, width:] += dot(attn.astype(jnp.bfloat16), g, NN)
+
+    def key_terms(first, masked):
+        part = pl.ds(first, batch)
+        q = qb[part].reshape(batch * rows, width)
+        g = gb[part].reshape(batch * rows, width)
+        attn, slope = weights(q, g)
+        if masked:
+            attn, slope = jnp.where(causal, attn, 0.0), jnp.where(causal, slope, 0.0)
+        return dot(slope.astype(jnp.bfloat16), q, NN), dot(attn.astype(jnp.bfloat16), g, NN)
+
+    for step in range(1, batch):
+        arrive(step)
+    acc[:, :width], acc[:, width:] = key_terms(0, True)
+
+    def more(n, carry):
+        for step in range(batch):
+            arrive(n * batch + step)
+        to_keys, to_values = key_terms(n * batch, False)
+        acc[:, :width] += to_keys
+        acc[:, width:] += to_values
+        return carry
+
+    if chips > batch:
+        lax.fori_loop(1, chips // batch, more, 0)
 
     sb[...] = acc[...].astype(jnp.bfloat16).reshape(group, share, 2 * width)
     swaps = []
@@ -193,8 +234,10 @@
     for offset, copy in enumerate(swaps, 1):
         copy.wait_recv()
         mine = mine + rb[offset].astype(jnp.float32)
-    dk_ref[0] = mine[:, :width].astype(dk_ref.dtype)
-    dv_ref[0] = mine[:, width:].astype(dv_ref.dtype)
+    dkvb[0] = mine[:, :width].astype(dkvb.dtype)
+    dkvb[1] = mine[:, width:].astype(dkvb.dtype)
+    dkv_out = pltpu.make_async_copy(dkvb, dkv_ref, out_sem.at[1])
+    dkv_out.start()
 
     for copy in swaps:
         copy.wait_send()
@@ -203,6 +246,8 @@
         def _():
             for copy in down(step):
                 copy.wait_send()
+    dq_out.wait()
+    dkv_out.wait()
 
 
 def body(queries, keys, values, out_grad, prefix_states):
@@ -213,14 +258,17 @@
     features = prefix_states.shape[1]
     share = rows // heads
     chunks = chunk_count(features)
+    whole = jax.ShapeDtypeStruct(queries.shape, jnp.bfloat16)
     half = jax.ShapeDtypeStruct((1, share, width), jnp.bfloat16)
     dma = pltpu.SemaphoreType.DMA
-    return pl.pallas_call(
+    grad_q, grad_kv = pl.pallas_call(
         kernel,
-        out_shape=(jax.ShapeDtypeStruct(queries.shape, jnp.bfloat16), half, half),
+        out_shape=(whole, jax.ShapeDtypeStruct((2, share, width), jnp.bfloat16)),
         in_specs=[pl.BlockSpec(memory_space=pl.ANY)] * 5,
-        out_specs=[pl.BlockSpec(memory_space=pltpu.VMEM)] * 3,
+        out_specs=[pl.BlockSpec(memory_space=pl.ANY)] * 2,
         scratch_shapes=[
+            pltpu.VMEM(queries.shape, jnp.bfloat16),
+            pltpu.VMEM((2, share, width), jnp.bfloat16),
             pltpu.VMEM((2, rows, width), jnp.bfloat16),
             pltpu.VMEM((2, rows, width), jnp.bfloat16),
             pltpu.VMEM((chips, rows, width), jnp.bfloat16),
@@ -232,6 +280,7 @@
             pltpu.VMEM((2 * rows, 2 * width), jnp.float32),
             pltpu.VMEM((group, share, 2 * width), jnp.bfloat16),
             pltpu.VMEM((group, share, 2 * width), jnp.bfloat16),
+            dma((2,)),
             dma((4,)),
             dma((chunks,)),
             dma((2,)),
@@ -249,6 +298,15 @@
         ),
         name="power_backward",
     )(queries, keys, values, out_grad, prefix_states)
+    return pl.pallas_call(
+        place,
+        out_shape=(whole, half, half),
+        in_specs=[pl.BlockSpec(memory_space=pl.ANY)] * 2,
+        out_specs=[pl.BlockSpec(memory_space=pl.ANY)] * 3,
+        scratch_shapes=[dma((3,))],
+        compiler_params=pltpu.CompilerParams(vmem_limit_bytes=63 * 1024 * 1024),
+        name="place_results",
+    )(grad_q, grad_kv)
 
 
 def solution(mesh):

time: 21.9 us -> 20.3 us (0.927)
  local copies, waits for them, and re-layouts: 3.96 us -> 0 us
  Pallas kernels: 17 us -> 19.5 us
    unnamed x3 -> x0, local copies, waits for them, and re-layouts: 3.96 us -> none
    pallas_call x1 -> x2, Pallas kernels: 17 us -> 19.5 us  [the longest x1 16.9 us: body(): pl.pallas_call(kernel, out_shape=(whole, jax.ShapeDtypeStruct((2, share,...]
where the time goes in v3:
time: 20.3 us; the launch traced here: 20.1 us
  Pallas kernels  19.5 us (96%)
  between operations  0.64 us (3%)
    pallas_call x1, Pallas kernels, body(): pl.pallas_call(kernel, out_shape=(whole, jax.ShapeDtypeStruct((2, share,...  16.9 us
    pallas_call x1, Pallas kernels, body(): pl.pallas_call(place, out_shape=(whole, half, half), in_specs=[pl.BlockSp...  2.62 us

profile of v3, /device:TPU:0, one launch (start us, length us, event | category | flops | bytes accessed | tf_op | source)
XLA Modules:
  0.0 20.1 jit_solution(16675095024826709513)
XLA Ops:
  0.6 16.9 %power_backward.1 = (bf16[1,128,128]{2,1,0:T(8,128)(2,1)}, bf16[2,32,128]{2,1,0:T(8,128)(2,1)}) custom-call(bf16[1,128,128]{2,1,0:T(8,128)(2,1)} %q_ref.1, bf16[128,128]{1,0:T(8,128)(2,1)} %k_ref.1, bf16[128,128]{1,0:T(8,128)(2,1)} %v_ref.1, bf16[1,128,128]{2,1,0:T(8,128)(2,1)} %g_ref.1, bf16[1,8256,128]{2,1,0:T(8,128)(2,1)} %p_ref.1), custom_call_target="tpu_custom_call" | custom-call | flops 270532608 | bytes 2113536 | tf_op jit(solution)/shard_map/power_backward/pallas_call | solution.py:264
  17.5 2.6 %place_results.1 = (bf16[1,128,128]{2,1,0:T(8,128)(2,1)}, bf16[1,32,128]{2,1,0:T(8,128)(2,1)}, bf16[1,32,128]{2,1,0:T(8,128)(2,1)}) custom-call(bf16[1,128,128]{2,1,0:T(8,128)(2,1)} %get-tuple-element.5.dq_in, bf16[2,32,128]{2,1,0:T(8,128)(2,1)} %get-tuple-element.6.dkv_in), custom_call_target="tpu_custom_call" | custom-call | tf_op jit(solution)/shard_map/place_results/pallas_call | solution.py:301

commit v4 on v3

--- a/solution.py
+++ b/solution.py
@@ -28,16 +28,24 @@
     return max(size for size in range(1, most + 1) if chips % size == 0)
 
 
-def place(dq_in, dkv_in, dq_out, dk_out, dv_out, sems):
-    copies = [
-        pltpu.make_async_copy(src, dst, sems.at[n])
-        for n, (src, dst) in enumerate(
-            ((dq_in, dq_out), (dkv_in.at[0], dk_out.at[0]), (dkv_in.at[1], dv_out.at[0]))
-        )
+def place(dq_in, dkv_in, dq_out, dk_out, dv_out, dq, dkv, sems):
+    fetch = [
+        pltpu.make_async_copy(dkv_in, dkv, sems.at[0]),
+        pltpu.make_async_copy(dq_in, dq, sems.at[1]),
     ]
-    for copy in copies:
+    put = [
+        pltpu.make_async_copy(dkv.at[0], dk_out.at[0], sems.at[2]),
+        pltpu.make_async_copy(dkv.at[1], dv_out.at[0], sems.at[3]),
+        pltpu.make_async_copy(dq, dq_out, sems.at[4]),
+    ]
+    for copy in fetch:
         copy.start()
-    for copy in copies:
+    fetch[0].wait()
+    put[0].start()
+    put[1].start()
+    fetch[1].wait()
+    put[2].start()
+    for copy in put:
         copy.wait()
 
 
@@ -80,33 +88,37 @@
 
     for offset in range(1, group):
         pl.semaphore_signal(barrier, inc=1, device_id=peer(offset), device_id_type=MESH)
-    for step in range(1, chips):
-        @pl.when(z + step < chips)
-        def _():
-            pl.semaphore_signal(
-                barrier, inc=1, device_id={"context": spot_at + 2 * step}, device_id_type=MESH
-            )
-    pl.semaphore_wait(barrier, group - 1 + z)
-
-    def down(step):
-        return [
-            pltpu.make_async_remote_copy(
-                src_ref=src.at[0],
-                dst_ref=dst.at[step],
-                send_sem=z_send.at[which, step],
-                recv_sem=z_recv.at[which, step],
-                device_id={"context": spot_at - 2 * step},
-                device_id_type=MESH,
-            )
-            for which, (src, dst) in enumerate(((q_ref, qb), (g_ref, gb)))
-        ]
-
-    for step in range(chips - 1, 0, -1):
-        @pl.when(z >= step)
-        def _():
-            for copy in down(step):
-                copy.start()
-
+
+    @pl.when(z + 1 < chips)
+    def _():
+        pl.semaphore_signal(barrier, inc=1, device_id={"context": spot_at + 2}, device_id_type=MESH)
+
+    pl.semaphore_wait(barrier, group - 1 + jnp.minimum(z, 1))
+
+    def hop(slot, which):
+        source, slots = ((q_ref, qb), (g_ref, gb))[which]
+        own = isinstance(slot, int) and slot == 0
+        return pltpu.make_async_remote_copy(
+            src_ref=source.at[0] if own else slots.at[slot],
+            dst_ref=slots.at[slot + 1],
+            send_sem=z_send.at[which, slot],
+            recv_sem=z_recv.at[which, slot],
+            device_id={"context": spot_at - 2},
+            device_id_type=MESH,
+        )
+
+    def start_own(which):
+        @pl.when(z > 0)
+        def _():
+            hop(0, which).start()
+
+    def forward(slot, which):
+        @pl.when((z > 0) & (z + slot < chips))
+        def _():
+            hop(slot - 1, which).wait_recv()
+            hop(slot, which).start()
+
+    start_own(0)
     kv = [
         pltpu.make_async_remote_copy(
             src_ref=src,
@@ -138,11 +150,16 @@
         fb[part, :] = dot(pb[part, :], g_own, NT)
         return carry
 
-    lax.fori_loop(0, chunks, expand, 0)
+    lax.fori_loop(0, chunks // 2, expand, 0)
+    start_own(1)
+    lax.fori_loop(chunks // 2, chunks, expand, 0)
+    between = {0: (1, 0), 3: (1, 1), 7: (2, 0), width // 8 - 1: (2, 1)}
     total = jnp.zeros((width, rows), jnp.float32)
     cross = []
     for tile in range(width // 8):
         length = width - 8 * tile
+        if tile in between and between[tile][0] < chips - 1:
+            forward(*between[tile])
 
         def one(r, total, tile=tile, length=length):
             i = 8 * tile + r
@@ -187,10 +204,10 @@
     causal = key_at <= jnp.where(query_at < rows, query_at + core * rows, 2 * rows)
 
     def arrive(step):
-        @pl.when(z + step < chips)
-        def _():
-            for copy in down(step):
-                copy.wait_recv()
+        @pl.when(z == 0)
+        def _():
+            for which in range(2):
+                hop(step - 1, which).wait_recv()
 
     def key_terms(first, masked):
         part = pl.ds(first, batch)
@@ -201,6 +218,13 @@
             attn, slope = jnp.where(causal, attn, 0.0), jnp.where(causal, slope, 0.0)
         return dot(slope.astype(jnp.bfloat16), q, NN), dot(attn.astype(jnp.bfloat16), g, NN)
 
+    def rest(slot, carry):
+        forward(slot, 0)
+        forward(slot, 1)
+        return carry
+
+    if chips > 4:
+        lax.fori_loop(3, chips - 1, rest, 0)
     for step in range(1, batch):
         arrive(step)
     acc[:, :width], acc[:, width:] = key_terms(0, True)
@@ -241,11 +265,11 @@
 
     for copy in swaps:
         copy.wait_send()
-    for step in range(1, chips):
-        @pl.when(z >= step)
-        def _():
-            for copy in down(step):
-                copy.wait_send()
+    for slot in range(chips - 1):
+        @pl.when((z > 0) & (z + slot < chips))
+        def _():
+            for which in range(2):
+                hop(slot, which).wait_send()
     dq_out.wait()
     dkv_out.wait()
 
@@ -303,7 +327,11 @@
         out_shape=(whole, half, half),
         in_specs=[pl.BlockSpec(memory_space=pl.ANY)] * 2,
         out_specs=[pl.BlockSpec(memory_space=pl.ANY)] * 3,
-        scratch_shapes=[dma((3,))],
+        scratch_shapes=[
+            pltpu.VMEM(queries.shape, jnp.bfloat16),
+            pltpu.VMEM((2, share, width), jnp.bfloat16),
+            dma((5,)),
+        ],
         compiler_params=pltpu.CompilerParams(vmem_limit_bytes=63 * 1024 * 1024),
         name="place_results",
     )(grad_q, grad_kv)

time: 20.3 us -> 22.9 us (1.13)
  Pallas kernels: 19.5 us -> 22 us
    pallas_call x1, Pallas kernels: 16.9 us -> 20.5 us  [body(): pl.pallas_call(kernel, out_shape=(whole, jax.ShapeDtypeStruct((2, share,...]
    pallas_call x1, Pallas kernels: 2.62 us -> 1.43 us  [body(): pl.pallas_call(place, out_shape=(whole, half, half), in_specs=[pl.BlockSp...]
where the time goes in v4:
time: 22.9 us; the launch traced here: 22.6 us
  Pallas kernels  22 us (96%)
  between operations  0.64 us (3%)
    pallas_call x1, Pallas kernels, body(): pl.pallas_call(kernel, out_shape=(whole, jax.ShapeDtypeStruct((2, share,...  20.5 us
    pallas_call x1, Pallas kernels, body(): pl.pallas_call(place, out_shape=(whole, half, half), in_specs=[pl.BlockSp...  1.43 us

profile of v4, /device:TPU:0, one launch (start us, length us, event | category | flops | bytes accessed | tf_op | source)
XLA Modules:
  0.0 22.6 jit_solution(742714959750151976)
XLA Ops:
  0.6 20.5 %power_backward.1 = (bf16[1,128,128]{2,1,0:T(8,128)(2,1)}, bf16[2,32,128]{2,1,0:T(8,128)(2,1)}) custom-call(bf16[1,128,128]{2,1,0:T(8,128)(2,1)} %q_ref.1, bf16[128,128]{1,0:T(8,128)(2,1)} %k_ref.1, bf16[128,128]{1,0:T(8,128)(2,1)} %v_ref.1, bf16[1,128,128]{2,1,0:T(8,128)(2,1)} %g_ref.1, bf16[1,8256,128]{2,1,0:T(8,128)(2,1)} %p_ref.1), custom_call_target="tpu_custom_call" | custom-call | flops 270532608 | bytes 2113536 | tf_op jit(solution)/shard_map/power_backward/pallas_call | solution.py:288
  21.2 1.4 %place_results.1 = (bf16[1,128,128]{2,1,0:T(8,128)(2,1)}, bf16[1,32,128]{2,1,0:T(8,128)(2,1)}, bf16[1,32,128]{2,1,0:T(8,128)(2,1)}) custom-call(bf16[1,128,128]{2,1,0:T(8,128)(2,1)} %get-tuple-element.5.dq_in, bf16[2,32,128]{2,1,0:T(8,128)(2,1)} %get-tuple-element.6.dkv_in), custom_call_target="tpu_custom_call" | custom-call | tf_op jit(solution)/shard_map/place_results/pallas_call | solution.py:325

commit v5 on v3

--- a/solution.py
+++ b/solution.py
@@ -291,7 +291,7 @@
             dma((group,)),
         ],
         compiler_params=pltpu.CompilerParams(
-            collective_id=0, has_side_effects=True, vmem_limit_bytes=63 * 1024 * 1024
+            collective_id=0, has_side_effects=True, vmem_limit_bytes=55168 * 1024
         ),
         cost_estimate=pl.CostEstimate(
             flops=2 * features * width * rows, bytes_accessed=2 * features * width, transcendentals=0
@@ -304,7 +304,7 @@
         in_specs=[pl.BlockSpec(memory_space=pl.ANY)] * 2,
         out_specs=[pl.BlockSpec(memory_space=pl.ANY)] * 3,
         scratch_shapes=[dma((3,))],
-        compiler_params=pltpu.CompilerParams(vmem_limit_bytes=63 * 1024 * 1024),
+        compiler_params=pltpu.CompilerParams(vmem_limit_bytes=55168 * 1024),
         name="place_results",
     )(grad_q, grad_kv)
 

time: 20.3 us -> 17.7 us (0.87)
  Pallas kernels: 19.5 us -> 17 us
    pallas_call x1, Pallas kernels: 2.62 us -> 0.65 us  [body(): pl.pallas_call(place, out_shape=(whole, half, half), in_specs=[pl.BlockSp...]
    pallas_call x1, Pallas kernels: 16.9 us -> 16.3 us  [body(): pl.pallas_call(kernel, out_shape=(whole, jax.ShapeDtypeStruct((2, share,...]
where the time goes in v5:
time: 17.7 us; the launch traced here: 17.6 us
  Pallas kernels  17 us (96%)
  between operations  0.64 us (4%)
    pallas_call x1, Pallas kernels, body(): pl.pallas_call(kernel, out_shape=(whole, jax.ShapeDtypeStruct((2, share,...  16.3 us
    pallas_call x1, Pallas kernels, body(): pl.pallas_call(place, out_shape=(whole, half, half), in_specs=[pl.BlockSp...  0.65 us

profile of v5, /device:TPU:0, one launch (start us, length us, event | category | flops | bytes accessed | tf_op | source)
XLA Modules:
  0.0 17.6 jit_solution(10721685530648869438)
XLA Ops:
  0.6 16.3 %power_backward.1 = (bf16[1,128,128]{2,1,0:T(8,128)(2,1)S(1)}, bf16[2,32,128]{2,1,0:T(8,128)(2,1)S(1)}) custom-call(bf16[1,128,128]{2,1,0:T(8,128)(2,1)} %q_ref.1, bf16[128,128]{1,0:T(8,128)(2,1)} %k_ref.1, bf16[128,128]{1,0:T(8,128)(2,1)} %v_ref.1, bf16[1,128,128]{2,1,0:T(8,128)(2,1)} %g_ref.1, bf16[1,8256,128]{2,1,0:T(8,128)(2,1)} %p_ref.1), custom_call_target="tpu_custom_call" | custom-call | flops 270532608 | bytes 2113536 | tf_op jit(solution)/shard_map/power_backward/pallas_call | solution.py:264
  16.9 0.6 %place_results.1 = (bf16[1,128,128]{2,1,0:T(8,128)(2,1)}, bf16[1,32,128]{2,1,0:T(8,128)(2,1)}, bf16[1,32,128]{2,1,0:T(8,128)(2,1)}) custom-call(bf16[1,128,128]{2,1,0:T(8,128)(2,1)S(1)} %get-tuple-element.5.dq_in, bf16[2,32,128]{2,1,0:T(8,128)(2,1)S(1)} %get-tuple-element.6.dkv_in), custom_call_target="tpu_custom_call" | custom-call | tf_op jit(solution)/shard_map/place_results/pallas_call | solution.py:301

commit v6 on v5

--- a/solution.py
+++ b/solution.py
@@ -22,10 +22,6 @@
         if features % (16 * count) == 0:
             return count
     return 1
-
-
-def block_batch(chips, most=4):
-    return max(size for size in range(1, most + 1) if chips % size == 0)
 
 
 def place(dq_in, dkv_in, dq_out, dk_out, dv_out, sems):
@@ -60,6 +56,20 @@
     chunks = chunk_count(features)
     chunk = features // chunks
 
+    barrier = pltpu.get_barrier_semaphore()
+
+    def peer(offset):
+        other = lax.rem(me + offset, group)
+        return {"query": other % heads, "context": 2 * z + other // heads}
+
+    for offset in range(1, group):
+        pl.semaphore_signal(barrier, inc=1, device_id=peer(offset), device_id_type=MESH)
+    for step in range(1, chips):
+        @pl.when(z + step < chips)
+        def _():
+            pl.semaphore_signal(
+                barrier, inc=1, device_id={"context": spot_at + 2 * step}, device_id_type=MESH
+            )
     loads = [
         pltpu.make_async_copy(q_ref.at[0], qb.at[0], local_sem.at[0]),
         pltpu.make_async_copy(g_ref.at[0], gb.at[0], local_sem.at[1]),
@@ -72,20 +82,6 @@
         part = pl.ds(n * chunk, chunk)
         pltpu.make_async_copy(p_ref.at[0, part], pb.at[part], p_sem.at[n]).start()
 
-    barrier = pltpu.get_barrier_semaphore()
-
-    def peer(offset):
-        other = lax.rem(me + offset, group)
-        return {"query": other % heads, "context": 2 * z + other // heads}
-
-    for offset in range(1, group):
-        pl.semaphore_signal(barrier, inc=1, device_id=peer(offset), device_id_type=MESH)
-    for step in range(1, chips):
-        @pl.when(z + step < chips)
-        def _():
-            pl.semaphore_signal(
-                barrier, inc=1, device_id={"context": spot_at + 2 * step}, device_id_type=MESH
-            )
     pl.semaphore_wait(barrier, group - 1 + z)
 
     def down(step):
@@ -120,11 +116,6 @@
     ]
     for copy in kv:
         copy.start()
-    for step in range(1, chips):
-        @pl.when(z + step >= chips)
-        def _():
-            qb[step] = jnp.zeros((rows, width), jnp.bfloat16)
-            gb[step] = jnp.zeros((rows, width), jnp.bfloat16)
     for load in loads:
         load.wait()
 
@@ -171,6 +162,14 @@
         score = dot(keys, q, NT)
         return scale * score * score, (2.0 * scale) * score * dot(vals, g, NT)
 
+    attn, slope = weights(q_own, g_own)
+    key_at = lax.broadcasted_iota(jnp.int32, (2 * rows, rows), 0)
+    query_at = lax.broadcasted_iota(jnp.int32, (2 * rows, rows), 1) + core * rows
+    causal = key_at <= query_at
+    attn = jnp.where(causal, attn, 0.0).astype(jnp.bfloat16)
+    slope = jnp.where(causal, slope, 0.0).astype(jnp.bfloat16)
+    acc[:, :width] = dot(slope, q_own, NN)
+    acc[:, width:] = dot(attn, g_own, NN)
     own_score = dot(q_own, kk[core], NT)
     own_slope = (2.0 * scale) * own_score * dot(g_own, vv[core], NT)
     own_causal = lax.broadcasted_iota(jnp.int32, (rows, rows), 1) <= lax.broadcasted_iota(
@@ -181,40 +180,16 @@
     dq_out = pltpu.make_async_copy(dqb, dq_ref, out_sem.at[0])
     dq_out.start()
 
-    batch = block_batch(chips)
-    key_at = lax.broadcasted_iota(jnp.int32, (2 * rows, batch * rows), 0)
-    query_at = lax.broadcasted_iota(jnp.int32, (2 * rows, batch * rows), 1)
-    causal = key_at <= jnp.where(query_at < rows, query_at + core * rows, 2 * rows)
-
-    def arrive(step):
-        @pl.when(z + step < chips)
-        def _():
-            for copy in down(step):
-                copy.wait_recv()
-
-    def key_terms(first, masked):
-        part = pl.ds(first, batch)
-        q = qb[part].reshape(batch * rows, width)
-        g = gb[part].reshape(batch * rows, width)
+    def later(step, carry):
+        for copy in down(step):
+            copy.wait_recv()
+        q, g = qb[step], gb[step]
         attn, slope = weights(q, g)
-        if masked:
-            attn, slope = jnp.where(causal, attn, 0.0), jnp.where(causal, slope, 0.0)
-        return dot(slope.astype(jnp.bfloat16), q, NN), dot(attn.astype(jnp.bfloat16), g, NN)
-
-    for step in range(1, batch):
-        arrive(step)
-    acc[:, :width], acc[:, width:] = key_terms(0, True)
-
-    def more(n, carry):
-        for step in range(batch):
-            arrive(n * batch + step)
-        to_keys, to_values = key_terms(n * batch, False)
-        acc[:, :width] += to_keys
-        acc[:, width:] += to_values
+        acc[:, :width] += dot(slope.astype(jnp.bfloat16), q, NN)
+        acc[:, width:] += dot(attn.astype(jnp.bfloat16), g, NN)
         return carry
 
-    if chips > batch:
-        lax.fori_loop(1, chips // batch, more, 0)
+    lax.fori_loop(1, chips - z, later, 0)
 
     sb[...] = acc[...].astype(jnp.bfloat16).reshape(group, share, 2 * width)
     swaps = []

time: 17.7 us -> 17.9 us (1.011)
  no operation moved by 1% of the time
where the time goes in v6:
time: 17.9 us; the launch traced here: 17.7 us
  Pallas kernels  17.1 us (96%)
  between operations  0.64 us (4%)
    pallas_call x1, Pallas kernels, body(): pl.pallas_call(kernel, out_shape=(whole, jax.ShapeDtypeStruct((2, share,...  16.4 us
    pallas_call x1, Pallas kernels, body(): pl.pallas_call(place, out_shape=(whole, half, half), in_specs=[pl.BlockSp...  0.65 us

profile of v6, /device:TPU:0, one launch (start us, length us, event | category | flops | bytes accessed | tf_op | source)
XLA Modules:
  0.0 17.7 jit_solution(14227312222190098405)
XLA Ops:
  0.6 16.4 %power_backward.1 = (bf16[1,128,128]{2,1,0:T(8,128)(2,1)S(1)}, bf16[2,32,128]{2,1,0:T(8,128)(2,1)S(1)}) custom-call(bf16[1,128,128]{2,1,0:T(8,128)(2,1)} %q_ref.1, bf16[128,128]{1,0:T(8,128)(2,1)} %k_ref.1, bf16[128,128]{1,0:T(8,128)(2,1)} %v_ref.1, bf16[1,128,128]{2,1,0:T(8,128)(2,1)} %g_ref.1, bf16[1,8256,128]{2,1,0:T(8,128)(2,1)} %p_ref.1), custom_call_target="tpu_custom_call" | custom-call | flops 270532608 | bytes 2113536 | tf_op jit(solution)/shard_map/power_backward/pallas_call | solution.py:239
  17.1 0.6 %place_results.1 = (bf16[1,128,128]{2,1,0:T(8,128)(2,1)}, bf16[1,32,128]{2,1,0:T(8,128)(2,1)}, bf16[1,32,128]{2,1,0:T(8,128)(2,1)}) custom-call(bf16[1,128,128]{2,1,0:T(8,128)(2,1)S(1)} %get-tuple-element.5.dq_in, bf16[2,32,128]{2,1,0:T(8,128)(2,1)S(1)} %get-tuple-element.6.dkv_in), custom_call_target="tpu_custom_call" | custom-call | tf_op jit(solution)/shard_map/place_results/pallas_call | solution.py:276

commit v7 on v5

--- a/solution.py
+++ b/solution.py
@@ -60,6 +60,20 @@
     chunks = chunk_count(features)
     chunk = features // chunks
 
+    barrier = pltpu.get_barrier_semaphore()
+
+    def peer(offset):
+        other = lax.rem(me + offset, group)
+        return {"query": other % heads, "context": 2 * z + other // heads}
+
+    for offset in range(1, group):
+        pl.semaphore_signal(barrier, inc=1, device_id=peer(offset), device_id_type=MESH)
+    for step in range(1, chips):
+        @pl.when(z + step < chips)
+        def _():
+            pl.semaphore_signal(
+                barrier, inc=1, device_id={"context": spot_at + 2 * step}, device_id_type=MESH
+            )
     loads = [
         pltpu.make_async_copy(q_ref.at[0], qb.at[0], local_sem.at[0]),
         pltpu.make_async_copy(g_ref.at[0], gb.at[0], local_sem.at[1]),
@@ -72,20 +86,6 @@
         part = pl.ds(n * chunk, chunk)
         pltpu.make_async_copy(p_ref.at[0, part], pb.at[part], p_sem.at[n]).start()
 
-    barrier = pltpu.get_barrier_semaphore()
-
-    def peer(offset):
-        other = lax.rem(me + offset, group)
-        return {"query": other % heads, "context": 2 * z + other // heads}
-
-    for offset in range(1, group):
-        pl.semaphore_signal(barrier, inc=1, device_id=peer(offset), device_id_type=MESH)
-    for step in range(1, chips):
-        @pl.when(z + step < chips)
-        def _():
-            pl.semaphore_signal(
-                barrier, inc=1, device_id={"context": spot_at + 2 * step}, device_id_type=MESH
-            )
     pl.semaphore_wait(barrier, group - 1 + z)
 
     def down(step):
@@ -101,11 +101,13 @@
             for which, (src, dst) in enumerate(((q_ref, qb), (g_ref, gb)))
         ]
 
-    for step in range(chips - 1, 0, -1):
-        @pl.when(z >= step)
-        def _():
-            for copy in down(step):
+    def send_to(chip):
+        @pl.when(z > chip)
+        def _():
+            for copy in down(z - chip):
                 copy.start()
+
+    send_to(0)
 
     kv = [
         pltpu.make_async_remote_copy(
@@ -139,10 +141,19 @@
         return carry
 
     lax.fori_loop(0, chunks, expand, 0)
+    send_to(1)
     total = jnp.zeros((width, rows), jnp.float32)
     cross = []
     for tile in range(width // 8):
         length = width - 8 * tile
+        if tile == 3:
+
+            def send_rest(chip, carry):
+                for copy in down(z - chip):
+                    copy.start()
+                return carry
+
+            lax.fori_loop(2, z, send_rest, 0)
 
         def one(r, total, tile=tile, length=length):
             i = 8 * tile + r

time: 17.7 us -> 17.2 us (0.972)
  Pallas kernels: 17 us -> 16.4 us
    pallas_call x1, Pallas kernels: 16.3 us -> 15.7 us  [body(): pl.pallas_call(kernel, out_shape=(whole, jax.ShapeDtypeStruct((2, share,...]
where the time goes in v7:
time: 17.2 us; the launch traced here: 17 us
  Pallas kernels  16.4 us (95%)
  between operations  0.64 us (4%)
    pallas_call x1, Pallas kernels, body(): pl.pallas_call(kernel, out_shape=(whole, jax.ShapeDtypeStruct((2, share,...  15.7 us
    pallas_call x1, Pallas kernels, body(): pl.pallas_call(place, out_shape=(whole, half, half), in_specs=[pl.BlockSp...  0.65 us

profile of v7, /device:TPU:0, one launch (start us, length us, event | category | flops | bytes accessed | tf_op | source)
XLA Modules:
  0.0 17.0 jit_solution(1099540209221533224)
XLA Ops:
  0.6 15.7 %power_backward.1 = (bf16[1,128,128]{2,1,0:T(8,128)(2,1)S(1)}, bf16[2,32,128]{2,1,0:T(8,128)(2,1)S(1)}) custom-call(bf16[1,128,128]{2,1,0:T(8,128)(2,1)} %q_ref.1, bf16[128,128]{1,0:T(8,128)(2,1)} %k_ref.1, bf16[128,128]{1,0:T(8,128)(2,1)} %v_ref.1, bf16[1,128,128]{2,1,0:T(8,128)(2,1)} %g_ref.1, bf16[1,8256,128]{2,1,0:T(8,128)(2,1)} %p_ref.1), custom_call_target="tpu_custom_call" | custom-call | flops 270532608 | bytes 2113536 | tf_op jit(solution)/shard_map/power_backward/pallas_call | solution.py:275
  16.4 0.6 %place_results.1 = (bf16[1,128,128]{2,1,0:T(8,128)(2,1)}, bf16[1,32,128]{2,1,0:T(8,128)(2,1)}, bf16[1,32,128]{2,1,0:T(8,128)(2,1)}) custom-call(bf16[1,128,128]{2,1,0:T(8,128)(2,1)S(1)} %get-tuple-element.5.dq_in, bf16[2,32,128]{2,1,0:T(8,128)(2,1)S(1)} %get-tuple-element.6.dkv_in), custom_call_target="tpu_custom_call" | custom-call | tf_op jit(solution)/shard_map/place_results/pallas_call | solution.py:312

commit v8 on v6

--- a/solution.py
+++ b/solution.py
@@ -22,6 +22,11 @@
         if features % (16 * count) == 0:
             return count
     return 1
+
+
+def later_batches(chips, most=3):
+    batch = max(1, min(most, chips - 1))
+    return batch, -(-(chips - 1) // batch)
 
 
 def place(dq_in, dkv_in, dq_out, dk_out, dv_out, sems):
@@ -97,11 +102,13 @@
             for which, (src, dst) in enumerate(((q_ref, qb), (g_ref, gb)))
         ]
 
-    for step in range(chips - 1, 0, -1):
-        @pl.when(z >= step)
+    def send_to(chip):
+        @pl.when(z > chip)
         def _():
-            for copy in down(step):
+            for copy in down(z - chip):
                 copy.start()
+
+    send_to(0)
 
     kv = [
         pltpu.make_async_remote_copy(
@@ -116,6 +123,11 @@
     ]
     for copy in kv:
         copy.start()
+    for step in range(1, qb.shape[0]):
+        @pl.when(z + step >= chips)
+        def _():
+            qb[step] = jnp.zeros((rows, width), jnp.bfloat16)
+            gb[step] = jnp.zeros((rows, width), jnp.bfloat16)
     for load in loads:
         load.wait()
 
@@ -130,10 +142,19 @@
         return carry
 
     lax.fori_loop(0, chunks, expand, 0)
+    send_to(1)
     total = jnp.zeros((width, rows), jnp.float32)
     cross = []
     for tile in range(width // 8):
         length = width - 8 * tile
+        if tile == 3:
+
+            def send_rest(chip, carry):
+                for copy in down(z - chip):
+                    copy.start()
+                return carry
+
+            lax.fori_loop(2, z, send_rest, 0)
 
         def one(r, total, tile=tile, length=length):
             i = 8 * tile + r
@@ -180,31 +201,48 @@
     dq_out = pltpu.make_async_copy(dqb, dq_ref, out_sem.at[0])
     dq_out.start()
 
-    def later(step, carry):
-        for copy in down(step):
-            copy.wait_recv()
-        q, g = qb[step], gb[step]
+    batch, batches = later_batches(chips)
+
+    def later(n, carry):
+        first = 1 + n * batch
+        for extra in range(batch):
+            @pl.when(z + first + extra < chips)
+            def _():
+                for copy in down(first + extra):
+                    copy.wait_recv()
+        part = pl.ds(first, batch)
+        q = qb[part].reshape(batch * rows, width)
+        g = gb[part].reshape(batch * rows, width)
         attn, slope = weights(q, g)
         acc[:, :width] += dot(slope.astype(jnp.bfloat16), q, NN)
         acc[:, width:] += dot(attn.astype(jnp.bfloat16), g, NN)
         return carry
 
-    lax.fori_loop(1, chips - z, later, 0)
+    if batches == 1:
+        later(0, 0)
+    else:
+        lax.fori_loop(0, batches, later, 0)
 
     sb[...] = acc[...].astype(jnp.bfloat16).reshape(group, share, 2 * width)
-    swaps = []
-    for offset in range(1, group):
-        other = lax.rem(me + offset, group)
-        copy = pltpu.make_async_remote_copy(
-            src_ref=sb.at[other],
+    def swap(dest, offset):
+        return pltpu.make_async_remote_copy(
+            src_ref=sb.at[dest],
             dst_ref=rb.at[offset],
             send_sem=x_send.at[offset],
             recv_sem=x_recv.at[offset],
-            device_id=peer(offset),
+            device_id={"query": dest % heads, "context": 2 * z + dest // heads},
             device_id_type=MESH,
         )
-        copy.start()
-        swaps.append(copy)
+
+    for head in range(heads):
+        for half in range(2):
+            dest = half * heads + head
+
+            @pl.when(me != dest)
+            def _():
+                swap(dest, lax.rem(dest - me + group, group)).start()
+
+    swaps = [swap(lax.rem(me + offset, group), offset) for offset in range(1, group)]
     mine = acc[pl.ds(pl.multiple_of(me * share, share), share), :]
     for offset, copy in enumerate(swaps, 1):
         copy.wait_recv()
@@ -233,6 +271,8 @@
     features = prefix_states.shape[1]
     share = rows // heads
     chunks = chunk_count(features)
+    batch, batches = later_batches(chips)
+    slots = 1 + batch * batches
     whole = jax.ShapeDtypeStruct(queries.shape, jnp.bfloat16)
     half = jax.ShapeDtypeStruct((1, share, width), jnp.bfloat16)
     dma = pltpu.SemaphoreType.DMA
@@ -246,8 +286,8 @@
             pltpu.VMEM((2, share, width), jnp.bfloat16),
             pltpu.VMEM((2, rows, width), jnp.bfloat16),
             pltpu.VMEM((2, rows, width), jnp.bfloat16),
-            pltpu.VMEM((chips, rows, width), jnp.bfloat16),
-            pltpu.VMEM((chips, rows, width), jnp.bfloat16),
+            pltpu.VMEM((slots, rows, width), jnp.bfloat16),
+            pltpu.VMEM((slots, rows, width), jnp.bfloat16),
             pltpu.VMEM((features, width), jnp.bfloat16),
             pltpu.VMEM((features, rows), jnp.float32),
             pltpu.VMEM((width, rows), jnp.float32),

time: 17.9 us -> 16.6 us (0.927)
  Pallas kernels: 17.1 us -> 15.8 us
    pallas_call x1, Pallas kernels: 16.4 us -> 15.2 us  [body(): pl.pallas_call(kernel, out_shape=(whole, jax.ShapeDtypeStruct((2, share,...]
where the time goes in v8:
time: 16.6 us; the launch traced here: 16.5 us
  Pallas kernels  15.8 us (95%)
  between operations  0.64 us (4%)
    pallas_call x1, Pallas kernels, body(): pl.pallas_call(kernel, out_shape=(whole, jax.ShapeDtypeStruct((2, share,...  15.2 us
    pallas_call x1, Pallas kernels, body(): pl.pallas_call(place, out_shape=(whole, half, half), in_specs=[pl.BlockSp...  0.65 us

profile of v8, /device:TPU:0, one launch (start us, length us, event | category | flops | bytes accessed | tf_op | source)
XLA Modules:
  0.0 16.5 jit_solution(4393520379457787126)
XLA Ops:
  0.6 15.2 %power_backward.1 = (bf16[1,128,128]{2,1,0:T(8,128)(2,1)S(1)}, bf16[2,32,128]{2,1,0:T(8,128)(2,1)S(1)}) custom-call(bf16[1,128,128]{2,1,0:T(8,128)(2,1)} %q_ref.1, bf16[128,128]{1,0:T(8,128)(2,1)} %k_ref.1, bf16[128,128]{1,0:T(8,128)(2,1)} %v_ref.1, bf16[1,128,128]{2,1,0:T(8,128)(2,1)} %g_ref.1, bf16[1,8256,128]{2,1,0:T(8,128)(2,1)} %p_ref.1), custom_call_target="tpu_custom_call" | custom-call | flops 270532608 | bytes 2113536 | tf_op jit(solution)/shard_map/power_backward/pallas_call | solution.py:279
  15.8 0.6 %place_results.1 = (bf16[1,128,128]{2,1,0:T(8,128)(2,1)}, bf16[1,32,128]{2,1,0:T(8,128)(2,1)}, bf16[1,32,128]{2,1,0:T(8,128)(2,1)}) custom-call(bf16[1,128,128]{2,1,0:T(8,128)(2,1)S(1)} %get-tuple-element.5.dq_in, bf16[2,32,128]{2,1,0:T(8,128)(2,1)S(1)} %get-tuple-element.6.dkv_in), custom_call_target="tpu_custom_call" | custom-call | tf_op jit(solution)/shard_map/place_results/pallas_call | solution.py:316

commit v9 on v8

--- a/solution.py
+++ b/solution.py
@@ -201,9 +201,39 @@
     dq_out = pltpu.make_async_copy(dqb, dq_ref, out_sem.at[0])
     dq_out.start()
 
+    def swap(dest, offset):
+        return pltpu.make_async_remote_copy(
+            src_ref=sb.at[dest],
+            dst_ref=rb.at[offset],
+            send_sem=x_send.at[offset],
+            recv_sem=x_recv.at[offset],
+            device_id={"query": dest % heads, "context": 2 * z + dest // heads},
+            device_id_type=MESH,
+        )
+
+    def send_half(part):
+        for dest in (0, heads):
+            offset = lax.rem(dest - me + group, group)
+
+            @pl.when(me != dest)
+            def _():
+                pltpu.make_async_remote_copy(
+                    src_ref=sb.at[dest, :, part],
+                    dst_ref=rb.at[offset, :, part],
+                    send_sem=x_send.at[offset],
+                    recv_sem=x_recv.at[offset],
+                    device_id={"query": 0, "context": 2 * z + dest // heads},
+                    device_id_type=MESH,
+                ).start()
+
+    def pack(part):
+        sb[:, :, part] = acc[:, part].astype(jnp.bfloat16).reshape(group, share, width)
+
+    key_half, value_half = pl.ds(0, width), pl.ds(width, width)
+
     batch, batches = later_batches(chips)
 
-    def later(n, carry):
+    def later(n, carry, last=False):
         first = 1 + n * batch
         for extra in range(batch):
             @pl.when(z + first + extra < chips)
@@ -214,27 +244,20 @@
         q = qb[part].reshape(batch * rows, width)
         g = gb[part].reshape(batch * rows, width)
         attn, slope = weights(q, g)
+        acc[:, width:] += dot(attn.astype(jnp.bfloat16), g, NN)
+        if last:
+            pack(value_half)
+            send_half(value_half)
         acc[:, :width] += dot(slope.astype(jnp.bfloat16), q, NN)
-        acc[:, width:] += dot(attn.astype(jnp.bfloat16), g, NN)
         return carry
 
-    if batches == 1:
-        later(0, 0)
-    else:
-        lax.fori_loop(0, batches, later, 0)
-
-    sb[...] = acc[...].astype(jnp.bfloat16).reshape(group, share, 2 * width)
-    def swap(dest, offset):
-        return pltpu.make_async_remote_copy(
-            src_ref=sb.at[dest],
-            dst_ref=rb.at[offset],
-            send_sem=x_send.at[offset],
-            recv_sem=x_recv.at[offset],
-            device_id={"query": dest % heads, "context": 2 * z + dest // heads},
-            device_id_type=MESH,
-        )
-
-    for head in range(heads):
+    if batches > 1:
+        lax.fori_loop(0, batches - 1, later, 0)
+    later(batches - 1, 0, True)
+
+    pack(key_half)
+    send_half(key_half)
+    for head in range(1, heads):
         for half in range(2):
             dest = half * heads + head
 

time: 16.6 us -> 16.7 us (level)
  no operation moved by 1% of the time
where the time goes in v9:
time: 16.7 us; the launch traced here: 16.5 us
  Pallas kernels  15.9 us (95%)
  between operations  0.64 us (4%)
    pallas_call x1, Pallas kernels, body(): pl.pallas_call(kernel, out_shape=(whole, jax.ShapeDtypeStruct((2, share,...  15.3 us
    pallas_call x1, Pallas kernels, body(): pl.pallas_call(place, out_shape=(whole, half, half), in_specs=[pl.BlockSp...  0.65 us

profile of v9, /device:TPU:0, one launch (start us, length us, event | category | flops | bytes accessed | tf_op | source)
XLA Modules:
  0.0 16.5 jit_solution(13827120052089287077)
XLA Ops:
  0.6 15.3 %power_backward.1 = (bf16[1,128,128]{2,1,0:T(8,128)(2,1)S(1)}, bf16[2,32,128]{2,1,0:T(8,128)(2,1)S(1)}) custom-call(bf16[1,128,128]{2,1,0:T(8,128)(2,1)} %q_ref.1, bf16[128,128]{1,0:T(8,128)(2,1)} %k_ref.1, bf16[128,128]{1,0:T(8,128)(2,1)} %v_ref.1, bf16[1,128,128]{2,1,0:T(8,128)(2,1)} %g_ref.1, bf16[1,8256,128]{2,1,0:T(8,128)(2,1)} %p_ref.1), custom_call_target="tpu_custom_call" | custom-call | flops 270532608 | bytes 2113536 | tf_op jit(solution)/shard_map/power_backward/pallas_call | solution.py:302
  15.9 0.6 %place_results.1 = (bf16[1,128,128]{2,1,0:T(8,128)(2,1)}, bf16[1,32,128]{2,1,0:T(8,128)(2,1)}, bf16[1,32,128]{2,1,0:T(8,128)(2,1)}) custom-call(bf16[1,128,128]{2,1,0:T(8,128)(2,1)S(1)} %get-tuple-element.5.dq_in, bf16[2,32,128]{2,1,0:T(8,128)(2,1)S(1)} %get-tuple-element.6.dkv_in), custom_call_target="tpu_custom_call" | custom-call | tf_op jit(solution)/shard_map/place_results/pallas_call | solution.py:339
